TPU v7x, 128 devices: a whole 4x4x4 slice. The times are simulated.
128 devices in a mesh: row: 8 (over y, core), col: 16 (over x, z).
Axes of the slice: x: 4, y: 4, z: 4, core: 2. Of those that a mesh axis runs over, the one named last changes fastest.
Arguments:
- factor: float32 [24, 1048576], P(None, ('row', 'col')), may hold values from -1.2 to 1.2
- prior: float32 [24, 1048576], P(None, ('row', 'col')), may hold values from -1.2 to 1.2
- tile_src: int32 [128, 384], P(('row', 'col')), may hold values from 0 to 63
- tile_dst: int32 [128, 384], P(('row', 'col')), may hold values from 0 to 63
- tile_count: int32 [128], P(('row', 'col')), may hold values from 96 to 384, as said below
- tile_vals: bfloat16 [49152, 128, 128], P(('row', 'col'))
- sep_idx: int32 [128, 4, 256], P(('row', 'col')), may hold values from 0 to 8191, as said below
- sep_count: int32 [128, 4], P(('row', 'col')), may hold values from 64 to 256, as said below
- couple: bfloat16 [128, 4, 256, 256], P(('row', 'col')), may hold values from -0.1875 to 0.1875
- masks: int32 [4], replicated, may hold values from 1 to 127, as said below
Outputs:
- new_factor: float32 [24, 1048576], P(None, ('row', 'col'))
- momentum: float32 [], replicated
- energy: float32 [], replicated
Inputs may be any that keep to these rules, and one draw needn't show every extreme that they name: `tile_count`: some partition has all 384 slots live; slots at or beyond a partition's count are padding. `sep_idx`: distinct within one partition and round. `sep_count`: in every round some partition has all 256 slots live. masks[0] is 127, masks[1] is 64 and the last round's mask is 1.
All inputs are finite; a program needn't handle non-finite values.
Results may differ from a plain program's by a relative error of at most 0.0031.
Values may be sent and summed in bfloat16 or wider, within the bound.
No kernel may reach another device: no remote copies, remote signals or barrier semaphores. Data moves between devices by JAX's collectives and lax.ppermute only.
A program may use at most 128 MiB of HBM per device.

v0:
```python
import jax
import jax.numpy as jnp
from jax import lax
from jax.sharding import PartitionSpec as P

TILE = 128
ITERS = 2


MOMENTUM_CAP = 0.9


def tile_product(packed, sources, targets, tile_vals, live_tiles, block_count):
    grouped = packed.reshape(packed.shape[0], block_count, packed.shape[1] // block_count)
    picked = jnp.take(grouped, sources, axis=1)
    products = jnp.einsum("rtk,tkc->trc", picked, tile_vals, preferred_element_type=jnp.float32)
    products = products * live_tiles[:, None, None]
    summed = jax.ops.segment_sum(products, targets, num_segments=block_count)
    return summed.transpose(1, 0, 2).reshape(packed.shape[0], packed.shape[1])


def pick_partner(piece, partner):
    owners = jnp.arange(piece.shape[0], dtype=jnp.int32)
    hit = owners == partner
    chosen = jnp.sum(jnp.where(hit[:, None, None], piece, jnp.zeros_like(piece)), axis=0)
    return chosen


def fetch_each(sent_block, partner):
    return pick_partner(
        lax.all_gather(sent_block[None], ("row", "col"), axis=0, tiled=True), partner
    )


def local(
    factor, prior, tile_src, tile_dst, tile_count, tile_vals, sep_idx, sep_count, couple, masks
):
    part_count = lax.axis_size(("row", "col"))
    own_index = lax.axis_index(("row", "col"))
    nodes_all = part_count * factor.shape[1]
    block_count = factor.shape[1] // TILE
    slot_count = sep_idx.shape[2]
    round_count = sep_idx.shape[1]
    live_tiles = (jnp.arange(tile_src.shape[1], dtype=jnp.int32) < tile_count[0]).astype(
        jnp.float32
    )
    partners = own_index ^ masks
    slot_range = jnp.arange(slot_count, dtype=jnp.int32)
    current = factor
    previous = prior
    beta = jnp.float32(0.5 * MOMENTUM_CAP)
    energy = jnp.float32(0.0)
    for iterate in range(ITERS):
        blend = current + beta * (current - previous)
        packed = blend.astype(jnp.bfloat16)
        applied = tile_product(packed, tile_src[0], tile_dst[0], tile_vals, live_tiles, block_count)
        sent_list = []
        for rounds in range(round_count):
            picked = jnp.take(packed, sep_idx[0, rounds], axis=1)
            keep = slot_range < sep_count[0, rounds]
            sent_list.append(jnp.where(keep[None, :], picked, jnp.zeros_like(picked)))
        received = [
            fetch_each(sent_list[rounds], partners[rounds]) for rounds in range(round_count)
        ]
        for rounds in range(round_count):
            extra = jnp.dot(received[rounds], couple[0, rounds], preferred_element_type=jnp.float32)
            keep = slot_range < sep_count[0, rounds]
            extra = jnp.where(keep[None, :], extra, jnp.zeros_like(extra))
            applied = applied.at[:, sep_idx[0, rounds]].add(extra)
        moved = blend + applied
        length = jnp.sqrt(jnp.sum(moved * moved, axis=0, keepdims=True))
        updated = moved / jnp.maximum(length, 1.0)
        change, total = lax.psum(
            (jnp.sum(applied * (updated - current)), jnp.sum(applied * updated)), ("row", "col")
        )
        energy = total / nodes_all
        beta = MOMENTUM_CAP * 0.5 * (1.0 + jnp.tanh(change / nodes_all))
        previous = current
        current = updated
    return (current, beta, energy)


def solution(mesh):
    in_specs = (
        P(None, ("row", "col")),
        P(None, ("row", "col")),
        P(("row", "col"), None),
        P(("row", "col"), None),
        P(("row", "col")),
        P(("row", "col"), None, None),
        P(("row", "col"), None, None),
        P(("row", "col"), None),
        P(("row", "col"), None, None, None),
        P(),
    )
    out_specs = (P(None, ("row", "col")), P(), P())
    return jax.shard_map(local, mesh=mesh, in_specs=in_specs, out_specs=out_specs, check_vma=False)
```

profile of v0, /device:TPU:1, one launch (start us, length us, event | category | flops | bytes accessed | tf_op | source)
XLA Modules:
  0.0 762.7 jit_solution(4418796748811676171)
XLA Ops:
  7.2 1.5 fusion.48
  10.2 3.6 copy.58
  13.8 2.7 copy.57
  16.5 4.1 fusion.15
  24.6 0.9 gather_fusion.2
  30.8 2.3 gather_fusion
  33.0 8.7 %broadcast_multiply_fusion.1 = f32[384,24,128]{2,1,0:T(8,128)} fusion(f32[384]{0:T(512)S(1)} %get-tuple-element.40, bf16[384,128,128]{2,1,0:T(8,128)(2,1)} %param.19, bf16[384,24,128]{2,1,0:T(8,128)(2,1)S(1)} %gather_fusion, pred[384]{0:T(512)(128)(4,1)S(1)} %get-tuple-element.41), kind=kOutput, calls=%fused_computation.34 | convolution fusion | flops 304349184 | bytes 19662720 | tf_op jit(solution)/shard_map/rtk,tkc->trc/dot_general | solution.py:16
  41.9 33.1 %scatter_fusion = f32[64,24,128]{2,1,0:T(8,128)S(1)} fusion(f32[64,24,128]{2,1,0:T(8,128)S(1)} %broadcast.129.clone, s32[384]{0:T(512)S(1)} %reduce.8, f32[384,24,128]{2,1,0:T(8,128)} %broadcast_multiply_fusion.1), kind=kCustom, calls=%fused_computation.10 | custom fusion | flops 1179648 | bytes 14157312 | tf_op jit(solution)/shard_map/scatter-add | solution.py:18
  75.0 2.6 copy.86
  80.8 9.3 %all-gather.23.cloned.1.call-done = bf16[3072,256]{1,0:T(8,128)(2,1)} async-done(((bf16[24,256]{1,0:T(8,128)(2,1)}), bf16[3072,256]{1,0:T(8,128)(2,1)}) %all-gather.23.cloned.1.call-update) | async-done | bytes 1572880 | tf_op jit(solution)/shard_map/all_gather | solution.py:31
  90.1 1.7 select_reduce_fusion.4
  91.9 62.7 %all-gather.21.cloned.1.call-done = bf16[3072,256]{1,0:T(8,128)(2,1)} async-done(((bf16[24,256]{1,0:T(8,128)(2,1)}), bf16[3072,256]{1,0:T(8,128)(2,1)}) %all-gather.21.cloned.1.call-update) | async-done | bytes 1572880 | tf_op jit(solution)/shard_map/all_gather | solution.py:31
  154.6 1.7 select_reduce_fusion.5
  156.3 62.7 %all-gather.19.cloned.1.call-done = bf16[3072,256]{1,0:T(8,128)(2,1)} async-done(((bf16[24,256]{1,0:T(8,128)(2,1)}), bf16[3072,256]{1,0:T(8,128)(2,1)}) %all-gather.19.cloned.1.call-update) | async-done | bytes 1572880 | tf_op jit(solution)/shard_map/all_gather | solution.py:31
  219.0 1.7 select_reduce_fusion.6
  221.2 62.7 %all-gather.17.cloned.1.call-done = bf16[3072,256]{1,0:T(8,128)(2,1)} async-done(((bf16[24,256]{1,0:T(8,128)(2,1)}), bf16[3072,256]{1,0:T(8,128)(2,1)}) %all-gather.17.cloned.1.call-update) | async-done | bytes 1572880 | tf_op jit(solution)/shard_map/all_gather | solution.py:31
  283.9 1.7 select_reduce_fusion.7
  286.2 5.9 scatter_fusion.1
  292.0 5.9 scatter_fusion.2
  297.9 5.9 scatter_fusion.3
  303.8 5.9 scatter_fusion.4
  309.7 6.0 multiply_reduce_fusion.4
  315.6 1.1 copy-done.1
  316.8 1.2 copy-done.3
  318.0 6.1 multiply_reduce_fusion.3
  324.1 62.3 %psum.21 = f32[]{:T(128)} all-reduce(f32[]{:T(128)} %get-tuple-element.21), channel_id=1, replica_groups=mesh['row'=8,'col'=16] {'row','col'}, use_global_device_ids=true, to_apply=%region_11.14 | all-reduce | flops 1 | bytes 8 | tf_op jit(solution)/shard_map/psum | solution.py:73
  387.1 3.9 fusion.13
  398.5 2.3 gather_fusion.5
  400.8 8.7 %broadcast_multiply_fusion = f32[384,24,128]{2,1,0:T(8,128)} fusion(f32[384]{0:T(512)S(1)} %get-tuple-element.40, bf16[384,128,128]{2,1,0:T(8,128)(2,1)} %param.19, bf16[384,24,128]{2,1,0:T(8,128)(2,1)S(1)} %gather_fusion.5, pred[384]{0:T(512)(128)(4,1)S(1)} %get-tuple-element.41), kind=kOutput, calls=%fused_computation.33 | convolution fusion | flops 304349184 | bytes 19662720 | tf_op jit(solution)/shard_map/rtk,tkc->trc/dot_general | solution.py:16
  409.6 33.1 %scatter_fusion.5 = f32[64,24,128]{2,1,0:T(8,128)S(1)} fusion(f32[64,24,128]{2,1,0:T(8,128)S(1)} %broadcast.129, s32[384]{0:T(512)S(1)} %reduce.8, f32[384,24,128]{2,1,0:T(8,128)} %broadcast_multiply_fusion), kind=kCustom, calls=%fused_computation.15 | custom fusion | flops 1179648 | bytes 14157312 | tf_op jit(solution)/shard_map/scatter-add | solution.py:18
  442.7 2.6 copy.87
  445.3 9.3 %all-gather.31.cloned.1.call-done = bf16[3072,256]{1,0:T(8,128)(2,1)} async-done(((bf16[24,256]{1,0:T(8,128)(2,1)}), bf16[3072,256]{1,0:T(8,128)(2,1)}) %all-gather.31.cloned.1.call-update) | async-done | bytes 1572880 | tf_op jit(solution)/shard_map/all_gather | solution.py:31
  454.6 1.7 select_reduce_fusion
  456.3 62.6 %all-gather.29.cloned.1.call-done = bf16[3072,256]{1,0:T(8,128)(2,1)} async-done(((bf16[24,256]{1,0:T(8,128)(2,1)}), bf16[3072,256]{1,0:T(8,128)(2,1)}) %all-gather.29.cloned.1.call-update) | async-done | bytes 1572880 | tf_op jit(solution)/shard_map/all_gather | solution.py:31
  518.9 1.7 select_reduce_fusion.1
  520.6 62.7 %all-gather.27.cloned.1.call-done = bf16[3072,256]{1,0:T(8,128)(2,1)} async-done(((bf16[24,256]{1,0:T(8,128)(2,1)}), bf16[3072,256]{1,0:T(8,128)(2,1)}) %all-gather.27.cloned.1.call-update) | async-done | bytes 1572880 | tf_op jit(solution)/shard_map/all_gather | solution.py:31
  583.3 1.7 select_reduce_fusion.2
  585.5 62.8 %all-gather.25.cloned.1.call-done = bf16[3072,256]{1,0:T(8,128)(2,1)} async-done(((bf16[24,256]{1,0:T(8,128)(2,1)}), bf16[3072,256]{1,0:T(8,128)(2,1)}) %all-gather.25.cloned.1.call-update) | async-done | bytes 1572880 | tf_op jit(solution)/shard_map/all_gather | solution.py:31
  648.3 1.7 select_reduce_fusion.3
  650.6 5.9 scatter_fusion.6
  656.5 5.9 scatter_fusion.7
  662.3 5.9 scatter_fusion.8
  668.2 5.9 scatter_fusion.9
  674.1 6.2 multiply_reduce_fusion.2
  680.3 0.9 copy-done.4
  681.2 5.2 multiply_reduce_fusion
  686.4 3.5 copy.83
  690.0 62.3 %all-reduce = (f32[]{:T(128)}, f32[]{:T(128)}) all-reduce(f32[]{:T(128)} %get-tuple-element.15, f32[]{:T(128)} %get-tuple-element.14), channel_id=1, replica_groups=mesh['row'=8,'col'=16] {'row','col'}, use_global_device_ids=true, to_apply=%region_23.26 | all-reduce | flops 2 | bytes 16 | tf_op jit(solution)/shard_map/psum | solution.py:73
  (105 shorter events, 22.8 us)
Async XLA Ops:
  7.2 6.7 copy-start.6
  7.2 83.0 %all-gather.23.cloned.1.call-start = ((), (), s32[]{:S(2)}) async-start(), calls=%async_computation.3 | async-start | bytes 1585152 | tf_op jit(solution)/shard_map/all_gather | solution.py:31
  16.5 13.3 %copy-start.8 = (s32[1,384]{1,0:T(1,128)S(1)}, s32[1,384]{1,0:T(1,128)}, u32[]{:S(2)}) copy-start(s32[1,384]{1,0:T(1,128)} %param.16) | copy-start | bytes 4612
  16.5 13.3 %copy-start.9 = (s32[1,384]{1,0:T(1,128)S(1)}, s32[1,384]{1,0:T(1,128)}, u32[]{:S(2)}) copy-start(s32[1,384]{1,0:T(1,128)} %param.17) | copy-start | bytes 4612
  22.2 132.4 %all-gather.21.cloned.1.call-start = ((), (), s32[]{:S(2)}) async-start(), calls=%async_computation.2 | async-start | bytes 1585152 | tf_op jit(solution)/shard_map/all_gather | solution.py:31
  24.5 194.5 %all-gather.19.cloned.1.call-start = ((), (), s32[]{:S(2)}) async-start(), calls=%async_computation.1 | async-start | bytes 1585152 | tf_op jit(solution)/shard_map/all_gather | solution.py:31
  26.8 257.1 %all-gather.17.cloned.1.call-start = ((), (), s32[]{:S(2)}) async-start(), calls=%async_computation | async-start | bytes 1585152 | tf_op jit(solution)/shard_map/all_gather | solution.py:31
  29.1 425.5 %all-gather.31.cloned.1.call-start = ((), (), s32[]{:S(2)}) async-start(), calls=%async_computation.7 | async-start | bytes 1585152 | tf_op jit(solution)/shard_map/all_gather | solution.py:31
  75.0 2.7 copy-start.10
  75.0 5.8 copy-start.7
  75.0 145.7 %copy-start.5 = (bf16[1,4,256,256]{3,2,1,0:T(8,128)(2,1)S(1)}, bf16[1,4,256,256]{3,2,1,0:T(8,128)(2,1)}, u32[]{:S(2)}) copy-start(bf16[1,4,256,256]{3,2,1,0:T(8,128)(2,1)} %param.22) | copy-start | bytes 1572868
  309.6 6.0 copy-start
  309.6 7.1 copy-start.1
  309.7 8.3 %copy-start.3 = (f32[24,8192]{0,1:T(8,128)S(1)}, f32[24,8192]{0,1:T(8,128)}, u32[]{:S(2)}) copy-start(f32[24,8192]{0,1:T(8,128)} %scatter_fusion.4) | copy-start | bytes 2359300
  392.6 126.3 %all-gather.29.cloned.1.call-start = ((), (), s32[]{:S(2)}) async-start(), calls=%async_computation.6 | async-start | bytes 1585152 | tf_op jit(solution)/shard_map/all_gather | solution.py:31
  394.2 189.1 %all-gather.27.cloned.1.call-start = ((), (), s32[]{:S(2)}) async-start(), calls=%async_computation.5 | async-start | bytes 1585152 | tf_op jit(solution)/shard_map/all_gather | solution.py:31
  395.8 252.5 %all-gather.25.cloned.1.call-start = ((), (), s32[]{:S(2)}) async-start(), calls=%async_computation.4 | async-start | bytes 1585152 | tf_op jit(solution)/shard_map/all_gather | solution.py:31
  674.1 6.2 copy-start.2
  674.1 7.1 copy-start.4
Sparse Core Ops, SparseCore 0:
  22.3 67.8 all-gather.22
  92.9 61.5 all-gather.20
  157.4 61.5 all-gather.18
  222.2 61.5 all-gather.16
  392.7 61.8 all-gather.30
  457.2 61.5 all-gather.28
  521.7 61.5 all-gather.26
  586.7 61.5 all-gather.24
where the time goes:
time: 765 us; the launch traced here: 763 us
  waiting for transfers between devices  395 us (52%)
  other arithmetic  169 us (22%)
  blocking collectives  125 us (16%)
  local copies, waits for them, and re-layouts  35.7 us (5%)
  between operations  19.4 us (3%)
  matrix products  18.7 us (2%)
    all_gather x8, waiting for transfers between devices, fetch_each(): lax.all_gather(sent_block[None], ('row', 'col'), axis=0, tiled=True)  395 us
    psum x2, blocking collectives, local(): lax.psum((jnp.sum(applied * (updated - current)), jnp.sum(applied * updat...  125 us
    scatter-add x2, other arithmetic, tile_product(): summed = jax.ops.segment_sum(products, targets, num_segments=block_count)  66.2 us
    scatter-add x8, other arithmetic, local(): applied = applied.at[:, sep_idx[0, rounds]].add(extra)  46.9 us
    dot_general x2, matrix products, tile_product(): jnp.einsum('rtk,tkc->trc', picked, tile_vals, preferred_element_type=jnp....  17.5 us
  transfers between devices with their start and end apart: 8, of which 8 were waited for; matrix products, arithmetic and copies ran while one was open for 16% of the time, Pallas kernels for 0%

commit v1 on v0

v1 whole, which is shorter than its diff:
```python
import jax
import jax.numpy as jnp
from jax import lax
from jax.experimental import pallas as pl
from jax.experimental.pallas import tpu as pltpu
from jax.sharding import PartitionSpec as P

TILE = 128
MOMENTUM_CAP = 0.9
BETA0 = 0.5 * MOMENTUM_CAP
AXES = ("row", "col")
VMEM_LIMIT = 48 * 1024 * 1024
SMEM = pl.BlockSpec(memory_space=pltpu.SMEM)
VMEM = pl.BlockSpec(memory_space=pltpu.VMEM)


def block_of(b):
    return pl.ds(pl.multiple_of(b * TILE, TILE), TILE)


def gather_columns(work, idx_ref, count_ref, outs):
    blocks, comps, _ = work.shape
    lane = lax.broadcasted_iota(jnp.int32, (1, TILE), 1)
    for k, out in enumerate(outs):
        slots = out.shape[1]
        if out.shape[0] > comps:
            out[...] = jnp.zeros_like(out)
        for h in range(slots // TILE):
            idx = idx_ref[k : k + 1, h * TILE : (h + 1) * TILE]
            live = lane + h * TILE < count_ref[0, k]
            home = jnp.broadcast_to(jnp.where(live, idx // TILE, -1), (comps, TILE))
            spot = jnp.broadcast_to(idx % TILE, (comps, TILE))

            def step(b, found, home=home, spot=spot):
                moved = jnp.take_along_axis(work[b], spot, axis=1, mode="promise_in_bounds")
                return jnp.where(home == b, moved, found)

            found = lax.fori_loop(0, blocks, step, jnp.zeros((comps, TILE), jnp.float32), unroll=8)
            rows = out.shape[0]
            if rows > comps:
                found = jnp.concatenate([found, jnp.zeros((rows - comps, TILE), jnp.float32)], axis=0)
            out[:, h * TILE : (h + 1) * TILE] = found.astype(out.dtype)


def prepare_kernel(factor, prior, idx_ref, count_ref, packed, *rest):
    outs, work = rest[:-1], rest[-1]
    blocks = packed.shape[0]
    comps = factor.shape[0]
    pad = jnp.zeros((packed.shape[1] - comps, TILE), jnp.float32)

    def step(b, _):
        f = factor[:, block_of(b)]
        blend = f + BETA0 * (f - prior[:, block_of(b)])
        work[b] = blend
        packed[b] = jnp.concatenate([blend, pad], axis=0).astype(packed.dtype)
        return 0

    lax.fori_loop(0, blocks, step, 0, unroll=4)
    gather_columns(work, idx_ref, count_ref, outs)


def prepare(factor, prior, sep_idx, sep_count):
    comps, nodes = factor.shape
    rounds, slots = sep_idx.shape
    rows = 32
    outs = pl.pallas_call(
        prepare_kernel,
        out_shape=[jax.ShapeDtypeStruct((nodes // TILE, rows, TILE), jnp.bfloat16)]
        + [jax.ShapeDtypeStruct((rows, slots), jnp.bfloat16)] * rounds,
        in_specs=[VMEM, VMEM, VMEM, SMEM],
        out_specs=[VMEM] * (1 + rounds),
        scratch_shapes=[pltpu.VMEM((nodes // TILE, comps, TILE), jnp.float32)],
        compiler_params=pltpu.CompilerParams(vmem_limit_bytes=VMEM_LIMIT),
        name="prepare",
    )(factor, prior, sep_idx, sep_count)
    return outs[0], list(outs[1:])


def tile_kernel(keep, group, src, dst, count, packed, vals, total):
    step = pl.program_id(0)
    chunk = vals.shape[0]
    spare = packed.shape[0]

    @pl.when(step == 0)
    def _():
        total[...] = jnp.zeros_like(total)

    def one(g, _):
        base = g * group
        first = step * chunk + base
        products = [
            jnp.dot(packed[src[0, first + j]], vals[base + j], preferred_element_type=jnp.float32)
            for j in range(group)
        ]
        for j in range(group):
            to = jnp.where(first + j < count[0], dst[0, first + j], spare)
            total[to] += products[j][:keep]
        return 0

    lax.fori_loop(0, chunk // group, one, 0)


def tile_product(packed, tile_src, tile_dst, tile_count, tile_vals, keep):
    blocks, rows, _ = packed.shape
    slots = tile_vals.shape[0]
    chunk, group = 32, 16

    def body(*refs):
        tile_kernel(keep, group, *refs)

    return pl.pallas_call(
        body,
        out_shape=jax.ShapeDtypeStruct((blocks + 1, keep, TILE), jnp.float32),
        grid_spec=pltpu.PrefetchScalarGridSpec(
            num_scalar_prefetch=3,
            grid=(slots // chunk,),
            in_specs=[
                pl.BlockSpec((blocks, rows, TILE), lambda i, *_: (0, 0, 0)),
                pl.BlockSpec((chunk, TILE, TILE), lambda i, *_: (i, 0, 0)),
            ],
            out_specs=pl.BlockSpec((blocks + 1, keep, TILE), lambda i, *_: (0, 0, 0)),
        ),
        compiler_params=pltpu.CompilerParams(vmem_limit_bytes=VMEM_LIMIT),
        cost_estimate=pl.CostEstimate(
            flops=2 * slots * rows * TILE * TILE,
            bytes_accessed=slots * TILE * TILE * 2 + blocks * rows * TILE * 8,
            transcendentals=0,
        ),
        name="tile_product",
    )(tile_src, tile_dst, tile_count, packed, tile_vals)


def scatter_rows(extra_rows, idx_smem, spread):
    rounds, slots = idx_smem.shape
    spread[...] = jnp.zeros_like(spread)
    for k in range(rounds):

        def step(c, _, k=k):
            at = [idx_smem[k, c * 8 + j] for j in range(8)]
            new = [
                spread[pl.ds(at[j], 1), :] + extra_rows[pl.ds(k * slots + c * 8 + j, 1), :]
                for j in range(8)
            ]
            for j in range(8):
                spread[pl.ds(at[j], 1), :] = new[j]
            return 0

        lax.fori_loop(0, slots // 8, step, 0, unroll=2)


def couple_rows(received, couple, count_ref, extra_rows, combine):
    for k, ref in enumerate(received):
        slots = ref.shape[1]
        extra = combine(jnp.dot(ref[...], couple[k], preferred_element_type=jnp.float32))
        slot = lax.broadcasted_iota(jnp.int32, extra.shape, 1)
        extra = jnp.where(slot < count_ref[0, k], extra, 0.0)
        fill = jnp.zeros((TILE - extra.shape[0], slots), jnp.float32)
        extra_rows[k * slots : (k + 1) * slots, :] = jnp.concatenate([extra, fill], axis=0).T


def fold(change, total):
    a = jnp.sum(change, axis=0, keepdims=True)
    b = jnp.sum(total, axis=0, keepdims=True)
    a = a + pltpu.roll(a, 64, 1)
    b = b + pltpu.roll(b, 64, 1)
    lane = lax.broadcasted_iota(jnp.int32, a.shape, 1)
    return jnp.where(lane < 64, a, b)


def first_kernel(factor, prior, total, r0, r1, r2, r3, couple, idx_ref, idx_smem, count_ref,
                 updated, packed, part, s0, s1, s2, s3, spread, extra_rows, work):
    comps = factor.shape[0]
    blocks = packed.shape[0]
    couple_rows((r0, r1, r2, r3), couple, count_ref, extra_rows, lambda e: e[:comps])
    scatter_rows(extra_rows, idx_smem, spread)

    def step(b, sums):
        f = factor[:, block_of(b)]
        blend = f + BETA0 * (f - prior[:, block_of(b)])
        applied = total[b] + spread[block_of(b), :].T[:comps]
        moved = blend + applied
        square = jnp.sum(moved * moved, axis=0, keepdims=True)
        u = moved * lax.rsqrt(jnp.maximum(square, 1.0))
        d = u - f
        updated[:, block_of(b)] = u
        both = jnp.concatenate([u + BETA0 * d, d], axis=0)
        work[b] = both
        packed[b] = both.astype(packed.dtype)
        return sums + applied * d

    sums = lax.fori_loop(0, blocks, step, jnp.zeros((comps, TILE), jnp.float32), unroll=2)
    part[...] = jnp.broadcast_to(fold(sums, sums), part.shape)
    gather_columns(work, idx_ref, count_ref, (s0, s1, s2, s3))


def finish_first(factor, prior, total, received, couple, sep_idx, sep_count, parts):
    comps, nodes = factor.shape
    rounds, slots = sep_idx.shape
    f32 = jnp.float32
    outs = pl.pallas_call(
        first_kernel,
        out_shape=[
            jax.ShapeDtypeStruct((comps, nodes), f32),
            jax.ShapeDtypeStruct((nodes // TILE, 2 * comps, TILE), jnp.bfloat16),
            jax.ShapeDtypeStruct((parts, TILE), f32),
        ]
        + [jax.ShapeDtypeStruct((2 * comps, slots), jnp.bfloat16)] * rounds,
        in_specs=[VMEM] * 9 + [SMEM, SMEM],
        out_specs=[VMEM] * (3 + rounds),
        scratch_shapes=[
            pltpu.VMEM((nodes, TILE), f32),
            pltpu.VMEM((rounds * slots, TILE), f32),
            pltpu.VMEM((nodes // TILE, 2 * comps, TILE), f32),
        ],
        compiler_params=pltpu.CompilerParams(vmem_limit_bytes=VMEM_LIMIT),
        name="finish_first",
    )(factor, prior, total, *received, couple, sep_idx, sep_idx, sep_count)
    return outs[0], outs[1], outs[2], list(outs[3:])


def beta_of(change, nodes_all):
    return MOMENTUM_CAP * 0.5 * (1.0 + jnp.tanh(change / nodes_all))


def last_kernel(nodes_all, current, factor, parts, total, r0, r1, r2, r3, couple, idx_smem, count_ref,
                updated, part, spread, extra_rows):
    comps = current.shape[0]
    blocks = total.shape[0] - 1
    lane = lax.broadcasted_iota(jnp.int32, (1, TILE), 1)
    summed = jnp.sum(parts[...], axis=0, keepdims=True)
    change = jnp.sum(jnp.where(lane < 64, summed, 0.0), axis=1, keepdims=True)
    beta = beta_of(change, nodes_all)
    gap = beta - BETA0
    couple_rows((r0, r1, r2, r3), couple, count_ref, extra_rows, lambda e: e[:comps] + gap * e[comps:])
    scatter_rows(extra_rows, idx_smem, spread)

    def step(b, sums):
        u = current[:, block_of(b)]
        blend = u + beta * (u - factor[:, block_of(b)])
        both = total[b]
        applied = both[:comps] + gap * both[comps:] + spread[block_of(b), :].T[:comps]
        moved = blend + applied
        square = jnp.sum(moved * moved, axis=0, keepdims=True)
        new = moved * lax.rsqrt(jnp.maximum(square, 1.0))
        updated[:, block_of(b)] = new
        return sums[0] + applied * (new - u), sums[1] + applied * new

    zero = jnp.zeros((comps, TILE), jnp.float32)
    sums = lax.fori_loop(0, blocks, step, (zero, zero), unroll=2)
    part[...] = jnp.broadcast_to(fold(*sums), part.shape)


def finish_last(current, factor, parts, total, received, couple, sep_idx, sep_count, nodes_all):
    comps, nodes = factor.shape
    rounds, slots = sep_idx.shape
    f32 = jnp.float32

    def body(*refs):
        last_kernel(nodes_all, *refs)

    return pl.pallas_call(
        body,
        out_shape=[
            jax.ShapeDtypeStruct((comps, nodes), f32),
            jax.ShapeDtypeStruct(parts.shape, f32),
        ],
        in_specs=[VMEM] * 9 + [SMEM, SMEM],
        out_specs=[VMEM] * 2,
        scratch_shapes=[
            pltpu.VMEM((nodes, TILE), f32),
            pltpu.VMEM((rounds * slots, TILE), f32),
        ],
        compiler_params=pltpu.CompilerParams(vmem_limit_bytes=VMEM_LIMIT),
        name="finish_last",
    )(current, factor, parts, total, *received, couple, sep_idx, sep_count)


def hop(value, mask, size):
    return lax.ppermute(value, AXES, [(i, i ^ mask) for i in range(size)])


def exchange(sent, masks, size, low):
    def stay(value):
        return value

    first = hop(sent[0], size - 1, size)
    second = hop(sent[1], size // 2, size)
    fourth = hop(sent[3], 1, size)
    mask = masks[2]
    third = lax.switch(
        mask % low, [stay] + [lambda v, m=m: hop(v, m, size) for m in range(1, low)], sent[2]
    )
    third = lax.switch(
        mask // low,
        [stay] + [lambda v, m=m: hop(v, m * low, size) for m in range(1, size // low)],
        third,
    )
    return [first, second, third, fourth]


def share(part):
    return lax.all_to_all(part, AXES, 0, 0, tiled=True)


def local(
    factor, prior, tile_src, tile_dst, tile_count, tile_vals, sep_idx, sep_count, couple, masks
):
    size = lax.axis_size(AXES)
    low = lax.axis_size("col")
    comps, nodes = factor.shape
    nodes_all = size * nodes
    idx, pairs = sep_idx[0], couple[0]
    packed, sent = prepare(factor, prior, idx, sep_count)
    received = exchange(sent, masks, size, low)
    total = tile_product(packed, tile_src, tile_dst, tile_count, tile_vals, comps)
    current, packed, part, sent = finish_first(
        factor, prior, total, received, pairs, idx, sep_count, size
    )
    parts = share(part)
    received = exchange(sent, masks, size, low)
    total = tile_product(packed, tile_src, tile_dst, tile_count, tile_vals, 2 * comps)
    updated, part = finish_last(
        current, factor, parts, total, received, pairs, idx, sep_count, nodes_all
    )
    summed = jnp.sum(share(part), axis=0)
    beta = beta_of(jnp.sum(summed[:64]), nodes_all)
    energy = jnp.sum(summed[64:]) / nodes_all
    return updated, beta, energy


def solution(mesh):
    in_specs = (
        P(None, ("row", "col")),
        P(None, ("row", "col")),
        P(("row", "col"), None),
        P(("row", "col"), None),
        P(("row", "col")),
        P(("row", "col"), None, None),
        P(("row", "col"), None, None),
        P(("row", "col"), None),
        P(("row", "col"), None, None, None),
        P(),
    )
    out_specs = (P(None, ("row", "col")), P(), P())
    return jax.shard_map(local, mesh=mesh, in_specs=in_specs, out_specs=out_specs, check_vma=False)
```

time: 765 us -> 133 us (0.17)
  waiting for transfers between devices: 395 us -> 9.53 us
  other arithmetic: 169 us -> 0.83 us
  blocking collectives: 125 us -> 14.9 us
  Pallas kernels: 0 us -> 54.7 us
  starting transfers between devices: 0.55 us -> 33.9 us
  local copies, waits for them, and re-layouts: 35.7 us -> 9.63 us
  matrix products: 18.7 us -> 0 us
  between operations: 19.4 us -> 7.67 us
    all_gather x8 -> x0, waiting for transfers between devices: 395 us -> none  [fetch_each(): lax.all_gather(sent_block[None], ('row', 'col'), axis=0, tiled=True)]
    psum x2 -> x0, blocking collectives: 125 us -> none  [local(): lax.psum((jnp.sum(applied * (updated - current)), jnp.sum(applied * updat...]
    scatter-add x10 -> x0, other arithmetic: 113 us -> none  [the longest x2 66.2 us: tile_product(): summed = jax.ops.segment_sum(products, targets, num_segments=block_count)]
    pallas_call x0 -> x5, Pallas kernels: none -> 54.7 us  [the longest x2 24.5 us: tile_product(): pl.pallas_call(body, out_shape=jax.ShapeDtypeStruct((blocks + 1, keep, TI...]
    reduce_sum x12 -> x2, other arithmetic: 37.3 us -> 0.83 us  [the longest x1 0.67 us: local(): energy = jnp.sum(summed[64:]) / nodes_all]
    ppermute x0 -> x10, starting transfers between devices: none -> 28.3 us  [hop(): return lax.ppermute(value, AXES, [(i, i ^ mask) for i in range(size)])]
    dot_general x10 -> x0, matrix products: 18.7 us -> none  [the longest x2 17.5 us: tile_product(): jnp.einsum('rtk,tkc->trc', picked, tile_vals, preferred_element_type=jnp....]
    all_to_all x0 -> x1, blocking collectives: none -> 14.9 us  [share(): return lax.all_to_all(part, AXES, 0, 0, tiled=True)]
  transfers between devices with their start and end apart: 8 -> 11, of which waited for: 8 -> 4; matrix products, arithmetic and copies ran while one was open for 16% -> 0% of each run, Pallas kernels for 0% -> 19%
where the time goes in v1:
time: 133 us; the launch traced here: 131 us
  Pallas kernels  54.7 us (41%)
  starting transfers between devices  33.9 us (25%)
  blocking collectives  14.9 us (11%)
  local copies, waits for them, and re-layouts  9.63 us (7%)
  waiting for transfers between devices  9.53 us (7%)
  between operations  7.67 us (6%)
    ppermute x10, starting transfers between devices, hop(): return lax.ppermute(value, AXES, [(i, i ^ mask) for i in range(size)])  28.3 us
    pallas_call x2, Pallas kernels, tile_product(): pl.pallas_call(body, out_shape=jax.ShapeDtypeStruct((blocks + 1, keep, TI...  24.5 us
    pallas_call x1, Pallas kernels, finish_first(): pl.pallas_call(first_kernel, out_shape=[jax.ShapeDtypeStruct((comps, node...  15.3 us
    all_to_all x1, blocking collectives, share(): return lax.all_to_all(part, AXES, 0, 0, tiled=True)  14.9 us
    ppermute x10, waiting for transfers between devices, hop(): return lax.ppermute(value, AXES, [(i, i ^ mask) for i in range(size)])  9.53 us
    unnamed x36, local copies, waits for them, and re-layouts  9.04 us
    pallas_call x1, Pallas kernels, finish_last(): pl.pallas_call(body, out_shape=[jax.ShapeDtypeStruct((comps, nodes), f32)...  7.85 us
    pallas_call x1, Pallas kernels, prepare(): pl.pallas_call(prepare_kernel, out_shape=[jax.ShapeDtypeStruct((nodes //...  6.95 us
  transfers between devices with their start and end apart: 11, of which 4 were waited for; matrix products, arithmetic and copies ran while one was open for 0% of the time, Pallas kernels for 19%

profile of v1, /device:TPU:1, one launch (start us, length us, event | category | flops | bytes accessed | tf_op | source)
XLA Modules:
  0.0 131.4 jit_solution(6788730269976649729)
XLA Ops:
  0.6 0.0 copy-start.12
  0.7 1.1 copy-done
  1.8 1.1 copy-done.2
  2.9 0.7 copy-done.9
  3.6 0.7 copy-done.15
  4.3 7.0 %prepare.1 = (bf16[64,32,128]{2,1,0:T(8,128)(2,1)S(1)}, bf16[32,256]{1,0:T(8,128)(2,1)S(1)}, bf16[32,256]{1,0:T(8,128)(2,1)S(1)}, bf16[32,256]{1,0:T(8,128)(2,1)S(1)}, bf16[32,256]{1,0:T(8,128)(2,1)S(1)}) custom-call(f32[24,8192]{1,0:T(8,128)S(1)} %copy-done, f32[24,8192]{1,0:T(8,128)S(1)} %copy-done.2, s32[4,256]{1,0:T(4,128)S(1)} %bitcast.13, ...), custom_call_target="tpu_custom_call" | custom-call | tf_op jit(solution)/shard_map/prepare/pallas_call | solution.py:66
  11.2 9.9 %collective-permute-start.44 = (bf16[32,256]{1,0:T(8,128)(2,1)S(1)}, bf16[32,256]{1,0:T(8,128)(2,1)S(1)}, u32[]{:S(2)}, u32[]{:S(2)}) collective-permute-start(bf16[32,256]{1,0:T(8,128)(2,1)S(1)} %get-tuple-element.118), channel_id=1, source_target_pairs={{0,127},{1,126},{2,125},{3,124},{4,123},{5,122},{6,121},{7,120},{8... | collective-permute-start | bytes 49160 | tf_op jit(solution)/shard_map/ppermute | solution.py:279
  21.1 0.3 collective-permute-start.45
  21.5 0.0 collective-permute-start.46
  22.1 0.0 copy-start.11
  22.1 0.7 copy-done.11
  22.8 0.7 copy-done.13
  23.5 12.0 %tile_product.2.total = f32[65,24,128]{2,1,0:T(8,128)S(1)} custom-call(s32[1,384]{1,0:T(1,128)S(1)} %copy-done.11, s32[1,384]{1,0:T(1,128)S(1)} %copy-done.13, s32[1]{0:T(128)S(6)} %copy.63.refs_2_, bf16[64,32,128]{2,1,0:T(8,128)(2,1)S(1)} %get-tuple-element.117.refs_3_, bf16[384,128,128]{2,1,0:T(8,128)(2,1)} %refs_4_.3), custom_call_target="tpu_custom_call" | custom-call | flops 402653184 | bytes 14680064 | tf_op jit(solution)/shard_map/tile_product/pallas_call | solution.py:111
  35.5 0.6 slice.10
  38.7 4.8 %conditional.4 = (bf16[32,256]{1,0:T(8,128)(2,1)S(1)}) conditional(s32[]{:T(128)} %clamp.9, bf16[32,256]{1,0:T(8,128)(2,1)S(1)} %get-tuple-element.120, bf16[32,256]{1,0:T(8,128)(2,1)S(1)} %get-tuple-element.120, bf16[32,256]{1,0:T(8,128)(2,1)S(1)} %get-tuple-element.120, ...), branch_computations={%region_0.1_spmd, %region_1.2_spmd, %region_2.3_spmd, %region_3.4_... | conditional | bytes 98352 | solution.py:290
  38.8 1.5 %collective-permute-start.12 = (bf16[32,256]{1,0:T(8,128)(2,1)S(1)}, bf16[32,256]{1,0:T(8,128)(2,1)S(1)}, u32[]{:S(2)}, u32[]{:S(2)}) collective-permute-start(bf16[32,256]{1,0:T(8,128)(2,1)S(1)} %param.13), channel_id=1, source_target_pairs={{0,13},{1,12},{2,15},{3,14},{4,9},{5,8},{6,11},{7,10},{8,5},{9,4},... | collective-permute-start | bytes 49160 | tf_op jit(solution)/shard_map/cond/branch_13_fun/ppermute | solution.py:279
  40.3 3.3 %collective-permute-done.12 = bf16[32,256]{1,0:T(8,128)(2,1)S(1)} collective-permute-done((bf16[32,256]{1,0:T(8,128)(2,1)S(1)}, bf16[32,256]{1,0:T(8,128)(2,1)S(1)}, u32[]{:S(2)}, u32[]{:S(2)}) %collective-permute-start.12) | collective-permute-done | bytes 16416 | tf_op jit(solution)/shard_map/cond/branch_13_fun/ppermute | solution.py:279
  43.5 4.5 %conditional.5 = (bf16[32,256]{1,0:T(8,128)(2,1)S(1)}) conditional(s32[]{:T(128)} %clamp.8, bf16[32,256]{1,0:T(8,128)(2,1)S(1)} %get-tuple-element.133, bf16[32,256]{1,0:T(8,128)(2,1)S(1)} %get-tuple-element.133, bf16[32,256]{1,0:T(8,128)(2,1)S(1)} %get-tuple-element.133, ...), branch_computations={%region_16.17_spmd, %region_17.18_spmd, %region_18.19_spmd, %regio... | conditional | bytes 98352 | solution.py:293
  43.5 3.1 %collective-permute-start.21 = (bf16[32,256]{1,0:T(8,128)(2,1)S(1)}, bf16[32,256]{1,0:T(8,128)(2,1)S(1)}, u32[]{:S(2)}, u32[]{:S(2)}) collective-permute-start(bf16[32,256]{1,0:T(8,128)(2,1)S(1)} %param.23), channel_id=1, source_target_pairs={{0,112},{1,113},{2,114},{3,115},{4,116},{5,117},{6,118},{7,119},{8... | collective-permute-start | bytes 49160 | tf_op jit(solution)/shard_map/cond/branch_7_fun/ppermute | solution.py:279
  46.6 1.4 %collective-permute-done.21 = bf16[32,256]{1,0:T(8,128)(2,1)S(1)} collective-permute-done((bf16[32,256]{1,0:T(8,128)(2,1)S(1)}, bf16[32,256]{1,0:T(8,128)(2,1)S(1)}, u32[]{:S(2)}, u32[]{:S(2)}) %collective-permute-start.21) | collective-permute-done | bytes 16416 | tf_op jit(solution)/shard_map/cond/branch_7_fun/ppermute | solution.py:279
  48.1 0.0 collective-permute-done.44.r0
  48.1 0.0 collective-permute-done.45.r1
  48.1 0.0 collective-permute-done.46.r3
  48.1 15.3 %finish_first.1 = (f32[24,8192]{1,0:T(8,128)S(1)}, bf16[64,48,128]{2,1,0:T(8,128)(2,1)S(1)}, f32[128,128]{1,0:T(8,128)}, bf16[48,256]{1,0:T(8,128)(2,1)S(1)}, bf...) custom-call(f32[24,8192]{1,0:T(8,128)S(1)} %copy-done.1, ...), custom_call_target="tpu_custom_call" | custom-call | tf_op jit(solution)/shard_map/finish_first/pallas_call | solution.py:200
  63.4 0.9 copy-done.5
  64.3 0.9 copy-done.7
  65.2 5.6 %all-to-all-start = ((f32[128,1,128]{2,1,0:T(1,128)}), f32[128,1,128]{2,1,0:T(1,128)S(1)}, u32[]{:S(2)}, u32[]{:S(2)}) async-start(f32[128,1,128]{2,1,0:T(1,128)} %bitcast.4), calls=%async_computation | async-start | bytes 131072 | tf_op jit(solution)/shard_map/all_to_all | solution.py:302
  70.9 8.1 %collective-permute-start.47 = (bf16[48,256]{1,0:T(8,128)(2,1)S(1)}, bf16[48,256]{1,0:T(8,128)(2,1)S(1)}, u32[]{:S(2)}, u32[]{:S(2)}) collective-permute-start(bf16[48,256]{1,0:T(8,128)(2,1)S(1)} %get-tuple-element.125), channel_id=1, source_target_pairs={{0,127},{1,126},{2,125},{3,124},{4,123},{5,122},{6,121},{7,120},{8... | collective-permute-start | bytes 73736 | tf_op jit(solution)/shard_map/ppermute | solution.py:279
  78.9 0.4 collective-permute-start.48
  79.4 0.0 collective-permute-start.49
  79.4 1.1 copy-done.8
  80.5 12.5 %tile_product.3.refs_3_ = f32[65,48,128]{2,1,0:T(8,128)S(1)} custom-call(s32[1,384]{1,0:T(1,128)S(1)} %copy-done.12, s32[1,384]{1,0:T(1,128)S(1)} %copy-done.14, s32[1]{0:T(128)S(6)} %copy.63.refs_2_, bf16[64,48,128]{2,1,0:T(8,128)(2,1)S(1)} %copy-done.8, bf16[384,128,128]{2,1,0:T(8,128)(2,1)} %refs_4_.3), custom_call_target="tpu_custom_call" | custom-call | flops 603979776 | bytes 15728640 | tf_op jit(solution)/shard_map/tile_product/pallas_call | solution.py:111
  93.0 5.1 %conditional.6 = (bf16[48,256]{1,0:T(8,128)(2,1)S(1)}) conditional(s32[]{:T(128)} %clamp.9, bf16[48,256]{1,0:T(8,128)(2,1)S(1)} %get-tuple-element.127, bf16[48,256]{1,0:T(8,128)(2,1)S(1)} %get-tuple-element.127, bf16[48,256]{1,0:T(8,128)(2,1)S(1)} %get-tuple-element.127, ...), branch_computations={%region_24.25_spmd, %region_25.26_spmd, %region_26.27_spmd, %regio... | conditional | bytes 147504 | solution.py:290
  93.3 1.5 %collective-permute-start.34 = (bf16[48,256]{1,0:T(8,128)(2,1)S(1)}, bf16[48,256]{1,0:T(8,128)(2,1)S(1)}, u32[]{:S(2)}, u32[]{:S(2)}) collective-permute-start(bf16[48,256]{1,0:T(8,128)(2,1)S(1)} %param.37), channel_id=1, source_target_pairs={{0,13},{1,12},{2,15},{3,14},{4,9},{5,8},{6,11},{7,10},{8,5},{9,4},... | collective-permute-start | bytes 73736 | tf_op jit(solution)/shard_map/cond/branch_13_fun/ppermute | solution.py:279
  94.8 3.3 %collective-permute-done.34 = bf16[48,256]{1,0:T(8,128)(2,1)S(1)} collective-permute-done((bf16[48,256]{1,0:T(8,128)(2,1)S(1)}, bf16[48,256]{1,0:T(8,128)(2,1)S(1)}, u32[]{:S(2)}, u32[]{:S(2)}) %collective-permute-start.34) | collective-permute-done | bytes 24608 | tf_op jit(solution)/shard_map/cond/branch_13_fun/ppermute | solution.py:279
  98.2 4.9 %conditional.7 = (bf16[48,256]{1,0:T(8,128)(2,1)S(1)}) conditional(s32[]{:T(128)} %clamp.8, bf16[48,256]{1,0:T(8,128)(2,1)S(1)} %get-tuple-element.135, bf16[48,256]{1,0:T(8,128)(2,1)S(1)} %get-tuple-element.135, bf16[48,256]{1,0:T(8,128)(2,1)S(1)} %get-tuple-element.135, ...), branch_computations={%region_40.41_spmd, %region_41.42_spmd, %region_42.43_spmd, %regio... | conditional | bytes 147504 | solution.py:293
  98.2 3.4 %collective-permute-start.43 = (bf16[48,256]{1,0:T(8,128)(2,1)S(1)}, bf16[48,256]{1,0:T(8,128)(2,1)S(1)}, u32[]{:S(2)}, u32[]{:S(2)}) collective-permute-start(bf16[48,256]{1,0:T(8,128)(2,1)S(1)} %param.47), channel_id=1, source_target_pairs={{0,112},{1,113},{2,114},{3,115},{4,116},{5,117},{6,118},{7,119},{8... | collective-permute-start | bytes 73736 | tf_op jit(solution)/shard_map/cond/branch_7_fun/ppermute | solution.py:279
  101.6 1.5 %collective-permute-done.43 = bf16[48,256]{1,0:T(8,128)(2,1)S(1)} collective-permute-done((bf16[48,256]{1,0:T(8,128)(2,1)S(1)}, bf16[48,256]{1,0:T(8,128)(2,1)S(1)}, u32[]{:S(2)}, u32[]{:S(2)}) %collective-permute-start.43) | collective-permute-done | bytes 24608 | tf_op jit(solution)/shard_map/cond/branch_7_fun/ppermute | solution.py:279
  103.1 0.0 collective-permute-done.47.refs_4_
  103.1 0.0 collective-permute-done.48.refs_5_
  103.1 0.0 collective-permute-done.49.refs_7_
  103.1 0.0 all-to-all-done
  103.1 0.0 copy-start.6
  103.1 1.1 copy-done.6
  104.2 7.9 %finish_last.1 = (f32[24,8192]{1,0:T(8,128)}, f32[128,128]{1,0:T(8,128)S(1)}) custom-call(f32[24,8192]{1,0:T(8,128)S(1)} %copy-done.6, f32[24,8192]{1,0:T(8,128)S(1)} %copy-done.1, f32[128,128]{1,0:T(8,128)S(1)} %bitcast.12, f32[65,48,128]{2,1,0:T(8,128)S(1)} %tile_product.3.refs_3_, bf16[48,256]{1,0:T(8,128)(2,1)S(1)} %collective-permute-done.47.refs_4_, ...), custom_call_target="tpu_custom_call" | custom-call | tf_op jit(solution)/shard_map/finish_last/pallas_call | solution.py:261
  112.1 14.9 %all_to_all.20 = f32[128,1,128]{2,1,0:T(1,128)S(1)} all-to-all(f32[128,1,128]{2,1,0:T(1,128)S(1)} %bitcast.17), channel_id=1, replica_groups=mesh['row'=8,'col'=16] {'row','col'}, dimensions={0} | all-to-all | bytes 131072 | tf_op jit(solution)/shard_map/all_to_all | solution.py:302
  127.0 0.2 reduce_sum.27
  127.2 0.7 slice_reduce_fusion
  (27 shorter events, 0.1 us)
Async XLA Ops:
  0.6 78.7 %copy-start.12 = (s32[1,384]{1,0:T(1,128)S(1)}, s32[1,384]{1,0:T(1,128)}, u32[]{:S(2)}) copy-start(s32[1,384]{1,0:T(1,128)} %refs_0_.3) | copy-start | bytes 4612
  0.6 1.1 copy-start
  1.8 1.1 copy-start.2
  2.9 0.7 copy-start.9
  3.6 0.7 copy-start.15
  4.3 43.8 %copy-start.1 = (f32[24,8192]{1,0:T(8,128)S(1)}, f32[24,8192]{1,0:T(8,128)}, u32[]{:S(2)}) copy-start(f32[24,8192]{1,0:T(8,128)} %refs_1_.5) | copy-start | bytes 2359300
  4.3 43.8 %copy-start.3 = (f32[24,8192]{1,0:T(8,128)S(1)}, f32[24,8192]{1,0:T(8,128)}, u32[]{:S(2)}) copy-start(f32[24,8192]{1,0:T(8,128)} %prior.3) | copy-start | bytes 2359300
  4.3 43.8 %copy-start.4 = (bf16[1,4,256,256]{3,2,1,0:T(8,128)(2,1)S(1)}, bf16[1,4,256,256]{3,2,1,0:T(8,128)(2,1)}, u32[]{:S(2)}) copy-start(bf16[1,4,256,256]{3,2,1,0:T(8,128)(2,1)} %param.66) | copy-start | bytes 1572868
  4.3 43.8 %copy-start.10 = (s32[1,4,256]{2,1,0:T(4,128)S(1)}, s32[1,4,256]{2,1,0:T(4,128)}, u32[]{:S(2)}) copy-start(s32[1,4,256]{2,1,0:T(4,128)} %param.64) | copy-start | bytes 12292
  11.2 36.8 %collective-permute-start.44 = (bf16[32,256]{1,0:T(8,128)(2,1)S(1)}, bf16[32,256]{1,0:T(8,128)(2,1)S(1)}, u32[]{:S(2)}, u32[]{:S(2)}) collective-permute-start(bf16[32,256]{1,0:T(8,128)(2,1)S(1)} %get-tuple-element.118), channel_id=1, source_target_pairs={{0,127},{1,126},{2,125},{3,124},{4,123},{5,122},{6,121},{7,120},{8... | collective-permute-start | bytes 49160 | tf_op jit(solution)/shard_map/ppermute | solution.py:279
  21.1 27.0 %collective-permute-start.45 = (bf16[32,256]{1,0:T(8,128)(2,1)S(1)}, bf16[32,256]{1,0:T(8,128)(2,1)S(1)}, u32[]{:S(2)}, u32[]{:S(2)}) collective-permute-start(bf16[32,256]{1,0:T(8,128)(2,1)S(1)} %get-tuple-element.119), channel_id=1, source_target_pairs={{0,64},{1,65},{2,66},{3,67},{4,68},{5,69},{6,70},{7,71},{8,72},{9,... | collective-permute-start | bytes 49160 | tf_op jit(solution)/shard_map/ppermute | solution.py:279
  21.5 26.6 %collective-permute-start.46 = (bf16[32,256]{1,0:T(8,128)(2,1)S(1)}, bf16[32,256]{1,0:T(8,128)(2,1)S(1)}, u32[]{:S(2)}, u32[]{:S(2)}) collective-permute-start(bf16[32,256]{1,0:T(8,128)(2,1)S(1)} %get-tuple-element.121), channel_id=1, source_target_pairs={{0,1},{1,0},{2,3},{3,2},{4,5},{5,4},{6,7},{7,6},{8,9},{9,8},{10,11... | collective-permute-start | bytes 49160 | tf_op jit(solution)/shard_map/ppermute | solution.py:279
  22.1 0.7 copy-start.11
  22.8 0.7 copy-start.13
  23.5 12.0 %copy-start.17 = (s32[4]{0:T(128)S(1)}, s32[4]{0:T(128)}, u32[]{:S(2)}) copy-start(s32[4]{0:T(128)} %param.67) | copy-start | bytes 52
  23.5 24.6 %copy-start.16 = (s32[1,4]{1,0:T(1,128)S(1)}, s32[1,4]{1,0:T(1,128)}, u32[]{:S(2)}) copy-start(s32[1,4]{1,0:T(1,128)} %refs_10_.1) | copy-start | bytes 52
  23.5 55.9 %copy-start.14 = (s32[1,384]{1,0:T(1,128)S(1)}, s32[1,384]{1,0:T(1,128)}, u32[]{:S(2)}) copy-start(s32[1,384]{1,0:T(1,128)} %refs_1_.4) | copy-start | bytes 4612
  38.8 4.8 %collective-permute-start.12 = (bf16[32,256]{1,0:T(8,128)(2,1)S(1)}, bf16[32,256]{1,0:T(8,128)(2,1)S(1)}, u32[]{:S(2)}, u32[]{:S(2)}) collective-permute-start(bf16[32,256]{1,0:T(8,128)(2,1)S(1)} %param.13), channel_id=1, source_target_pairs={{0,13},{1,12},{2,15},{3,14},{4,9},{5,8},{6,11},{7,10},{8,5},{9,4},... | collective-permute-start | bytes 49160 | tf_op jit(solution)/shard_map/cond/branch_13_fun/ppermute | solution.py:279
  43.5 4.5 %collective-permute-start.21 = (bf16[32,256]{1,0:T(8,128)(2,1)S(1)}, bf16[32,256]{1,0:T(8,128)(2,1)S(1)}, u32[]{:S(2)}, u32[]{:S(2)}) collective-permute-start(bf16[32,256]{1,0:T(8,128)(2,1)S(1)} %param.23), channel_id=1, source_target_pairs={{0,112},{1,113},{2,114},{3,115},{4,116},{5,117},{6,118},{7,119},{8... | collective-permute-start | bytes 49160 | tf_op jit(solution)/shard_map/cond/branch_7_fun/ppermute | solution.py:279
  63.4 0.9 copy-start.5
  64.3 0.9 copy-start.7
  65.2 37.9 %all-to-all-start = ((f32[128,1,128]{2,1,0:T(1,128)}), f32[128,1,128]{2,1,0:T(1,128)S(1)}, u32[]{:S(2)}, u32[]{:S(2)}) async-start(f32[128,1,128]{2,1,0:T(1,128)} %bitcast.4), calls=%async_computation | async-start | bytes 131072 | tf_op jit(solution)/shard_map/all_to_all | solution.py:302
  70.9 32.2 %collective-permute-start.47 = (bf16[48,256]{1,0:T(8,128)(2,1)S(1)}, bf16[48,256]{1,0:T(8,128)(2,1)S(1)}, u32[]{:S(2)}, u32[]{:S(2)}) collective-permute-start(bf16[48,256]{1,0:T(8,128)(2,1)S(1)} %get-tuple-element.125), channel_id=1, source_target_pairs={{0,127},{1,126},{2,125},{3,124},{4,123},{5,122},{6,121},{7,120},{8... | collective-permute-start | bytes 73736 | tf_op jit(solution)/shard_map/ppermute | solution.py:279
  78.9 24.2 %collective-permute-start.48 = (bf16[48,256]{1,0:T(8,128)(2,1)S(1)}, bf16[48,256]{1,0:T(8,128)(2,1)S(1)}, u32[]{:S(2)}, u32[]{:S(2)}) collective-permute-start(bf16[48,256]{1,0:T(8,128)(2,1)S(1)} %get-tuple-element.126), channel_id=1, source_target_pairs={{0,64},{1,65},{2,66},{3,67},{4,68},{5,69},{6,70},{7,71},{8,72},{9,... | collective-permute-start | bytes 73736 | tf_op jit(solution)/shard_map/ppermute | solution.py:279
  79.4 23.7 %collective-permute-start.49 = (bf16[48,256]{1,0:T(8,128)(2,1)S(1)}, bf16[48,256]{1,0:T(8,128)(2,1)S(1)}, u32[]{:S(2)}, u32[]{:S(2)}) collective-permute-start(bf16[48,256]{1,0:T(8,128)(2,1)S(1)} %get-tuple-element.128), channel_id=1, source_target_pairs={{0,1},{1,0},{2,3},{3,2},{4,5},{5,4},{6,7},{7,6},{8,9},{9,8},{10,11... | collective-permute-start | bytes 73736 | tf_op jit(solution)/shard_map/ppermute | solution.py:279
  79.4 1.1 copy-start.8
  93.3 4.9 %collective-permute-start.34 = (bf16[48,256]{1,0:T(8,128)(2,1)S(1)}, bf16[48,256]{1,0:T(8,128)(2,1)S(1)}, u32[]{:S(2)}, u32[]{:S(2)}) collective-permute-start(bf16[48,256]{1,0:T(8,128)(2,1)S(1)} %param.37), channel_id=1, source_target_pairs={{0,13},{1,12},{2,15},{3,14},{4,9},{5,8},{6,11},{7,10},{8,5},{9,4},... | collective-permute-start | bytes 73736 | tf_op jit(solution)/shard_map/cond/branch_13_fun/ppermute | solution.py:279
  98.2 4.9 %collective-permute-start.43 = (bf16[48,256]{1,0:T(8,128)(2,1)S(1)}, bf16[48,256]{1,0:T(8,128)(2,1)S(1)}, u32[]{:S(2)}, u32[]{:S(2)}) collective-permute-start(bf16[48,256]{1,0:T(8,128)(2,1)S(1)} %param.47), channel_id=1, source_target_pairs={{0,112},{1,113},{2,114},{3,115},{4,116},{5,117},{6,118},{7,119},{8... | collective-permute-start | bytes 73736 | tf_op jit(solution)/shard_map/cond/branch_7_fun/ppermute | solution.py:279
  103.1 1.1 copy-start.6
